TPU v7x, 32 devices: a whole 2x2x4 slice. The times are simulated.
32 devices in a mesh: tgt: 8 (over z, x), src: 4 (over y, core).
Axes of the slice: x: 2, y: 2, z: 4, core: 2. Of those that a mesh axis runs over, the one named last changes fastest.
Arguments:
- points: bfloat16 [65536, 256], P(('tgt', 'src')), may hold values from -0.4 to 0.4
- weights: bfloat16 [65536, 64], P(('tgt', 'src')), may hold values from -6 to 6
- near_list: int32 [512, 16], P(('tgt', 'src')), may hold values from -1 to 63, as said below
- far_list: int32 [512, 3, 4], P('tgt', None, 'src'), may hold values from -1 to 31, as said below
- skel_index: int32 [224, 256], P(('tgt', 'src')), may hold values from 0 to 2047, as said below
- equiv_weights: bfloat16 [224, 256, 64], P(('tgt', 'src')), may hold values from -6 to 6
Outputs:
- potential: float32 [65536, 64], P(('tgt', 'src'))
Inputs may be any that keep to these rules, and one draw needn't show every extreme that they name: `near_list`: row b lists blocks of b's group of 64 blocks by their index within the group: first b itself, then distinct other blocks; after a row's live entries all are -1; every row has 4 or more live entries. `far_list`: entry [b, l, c] is -1 or a level-l node owned by a device of src index c, numbered as the owner's tgt index times (16 // (4 * 2 ** l)) plus the node's number among the owner's level-l nodes. `skel_index`: Level-l nodes of a device cover 4 * 128 * 2 ** l consecutive points of that device each, in order; a node's 256 entries are increasing indices of the device's points inside the node.
All inputs are finite; a program needn't handle non-finite values.
Results may differ from a plain program's by a relative error of at most 0.0023.
Values may be sent and summed in bfloat16 or wider, within the bound.
A program may use at most 192 MiB of HBM per device.

v0:
```python
import jax
import jax.numpy as jnp
from jax import lax
from jax.sharding import PartitionSpec as P

E = 256
WCOL = 64
BLK = 128
RANK = 256
NEAR = 16
LEVELS = 3


kernel_rate = 2.0


def square_norms(values):
    return jnp.sum(jnp.square(values.astype(jnp.float32)), axis=-1)


def tile_kernel(targets, target_norms, sources, source_norms, live_mask):
    dot_terms = jnp.einsum("bie,bse->bis", targets, sources, preferred_element_type=jnp.float32)
    sq_dist = target_norms[:, :, None] + source_norms[:, None, :] - 2.0 * dot_terms
    return jnp.where(live_mask[:, None, :], jnp.exp(-kernel_rate * sq_dist), 0.0).astype(
        jnp.bfloat16
    )


def apply_tile(kernel, source_weights):
    return jnp.einsum("bis,bsw->biw", kernel, source_weights, preferred_element_type=jnp.float32)


def shards(points, weights, near_list, far_list, skel_index, equiv_weights):
    point_dev = points.shape[0]
    blk_dev = point_dev // BLK
    src_size = lax.axis_size("src")
    src_index = lax.axis_index("src")
    group_blocks = src_size * blk_dev
    node_dev = skel_index.shape[0]
    level_nodes = [blk_dev // (4 * 2**tree_level) for tree_level in range(LEVELS)]
    level_start = [sum(level_nodes[:tree_level]) for tree_level in range(LEVELS)]
    group_pts, group_wts = (
        lax.all_gather(points, "src", axis=0, tiled=True),
        lax.all_gather(weights, "src", axis=0, tiled=True),
    )
    tgt_blocks = group_pts.reshape(group_blocks, BLK, E)
    tgt_norms = square_norms(group_pts).reshape(group_blocks, BLK)
    wt_blocks = group_wts.reshape(group_blocks, BLK, WCOL)
    skel_pts = jnp.take(points, skel_index.reshape(-1), axis=0).reshape(node_dev, RANK, E)
    panels = []
    all_pts, all_wts = (
        lax.all_gather(skel_pts, "tgt", axis=0, tiled=True),
        lax.all_gather(equiv_weights, "tgt", axis=0, tiled=True),
    )
    all_norms = square_norms(all_pts)
    for tree_level in range(LEVELS):
        panels.append((all_pts, all_norms, all_wts, node_dev, level_start[tree_level]))
    own_blocks = points.reshape(blk_dev, BLK, E)
    own_norms = lax.dynamic_slice_in_dim(tgt_norms, src_index * blk_dev, blk_dev, 0)
    near_live = near_list >= 0
    near_index = jnp.where(near_live, near_list, 0)
    sources = tgt_blocks[near_index].reshape(blk_dev, NEAR * BLK, E)
    source_norms = tgt_norms[near_index].reshape(blk_dev, NEAR * BLK)
    source_wts = wt_blocks[near_index].reshape(blk_dev, NEAR * BLK, WCOL)
    kernel = tile_kernel(
        own_blocks, own_norms, sources, source_norms, jnp.repeat(near_live, BLK, axis=1)
    )
    own_near = apply_tile(kernel, source_wts).reshape(point_dev, WCOL)
    row_count = src_size * point_dev
    block_count = row_count // BLK
    far_total = jnp.zeros((block_count, BLK, WCOL), jnp.float32)
    for tree_level in range(LEVELS):
        panel_pts, panel_norms, panel_wts, stride_rows, offset_rows = panels[tree_level]
        level_count = level_nodes[tree_level]
        far_entry = far_list[:, tree_level, 0]
        far_live = far_entry >= 0
        far_entry = jnp.where(far_live, far_entry, 0)
        panel_rows = far_entry // level_count * stride_rows + offset_rows + far_entry % level_count
        kernel = tile_kernel(
            tgt_blocks,
            tgt_norms,
            panel_pts[panel_rows],
            panel_norms[panel_rows],
            jnp.broadcast_to(far_live[:, None], (block_count, RANK)),
        )
        far_total = far_total + apply_tile(kernel, panel_wts[panel_rows])
    whole_term = lax.psum(far_total.reshape(row_count, WCOL), "src")
    mine_term = lax.dynamic_slice_in_dim(whole_term, src_index * point_dev, point_dev, 0)
    mine_term = mine_term + own_near
    return mine_term


def solution(mesh):
    in_specs = (
        P(("tgt", "src"), None),
        P(("tgt", "src"), None),
        P(("tgt", "src"), None),
        P("tgt", None, "src"),
        P(("tgt", "src"), None),
        P(("tgt", "src"), None, None),
    )
    out_specs = P(("tgt", "src"), None)
    return jax.shard_map(shards, mesh=mesh, in_specs=in_specs, out_specs=out_specs, check_vma=False)
```

profile of v0, /device:TPU:1, one launch (start us, length us, event | category | flops | bytes accessed | tf_op | source)
XLA Modules:
  0.0 343.8 jit_solution(9928340218867710125)
XLA Ops:
  9.5 5.5 %gather_fusion = bf16[1792,256]{1,0:T(8,128)(2,1)S(1)} fusion(bf16[2048,256]{1,0:T(8,128)(2,1)} %param.6, s32[2048]{0:T(1024)S(1)} %pad_clamp_fusion), kind=kCustom, calls=%fused_computation | custom fusion | bytes 1842176 | tf_op jit(solution)/shard_map/jit(_take)/gather | solution.py:49
  16.8 11.4 %all-gather.11.cloned.1.call-done = bf16[8192,64]{0,1:T(8,128)(2,1)} async-done(((bf16[2048,64]{0,1:T(8,128)(2,1)}), bf16[8192,64]{0,1:T(8,128)(2,1)}) %all-gather.11.cloned.1.call-update) | async-done | bytes 1048592 | tf_op jit(solution)/shard_map/all_gather | solution.py:44
  29.7 3.0 gather_fusion.12
  32.8 6.8 %copy.25 = bf16[256,128,64]{1,0,2:T(8,128)(2,1)} copy(bf16[256,128,64]{1,2,0:T(8,128)(2,1)} %gather_fusion.12) | data formatting | bytes 8388608 | tf_op jit(solution)/shard_map/gather | solution.py:64
  39.6 7.3 %reshape.319 = bf16[16,2048,64]{1,0,2:T(8,128)(2,1)} reshape(bf16[256,128,64]{1,0,2:T(8,128)(2,1)} %copy.25) | data formatting | bytes 8388608 | tf_op jit(solution)/shard_map/reshape | solution.py:64
  46.9 28.3 %all-gather.9.cloned.1.call-done = bf16[56,256,64]{1,2,0:T(8,128)(2,1)} async-done(((bf16[7,256,64]{1,2,0:T(8,128)(2,1)}), bf16[56,256,64]{1,2,0:T(8,128)(2,1)}) %all-gather.9.cloned.1.call-update) | async-done | bytes 1835024 | tf_op jit(solution)/shard_map/all_gather | solution.py:53
  75.2 3.6 %gather_fusion.6 = bf16[64,256,64]{1,2,0:T(8,128)(2,1)} fusion(bf16[56,256,64]{1,2,0:T(8,128)(2,1)} %all-gather.9.cloned.1.call-done, s32[1024]{0:T(1024)S(1)} %get-tuple-element.12), kind=kCustom, calls=%fused_computation.6 | custom fusion | bytes 4194560 | tf_op jit(solution)/shard_map/gather | solution.py:86
  78.9 2.1 gather_fusion.3
  80.9 2.0 gather_fusion.9
  82.9 28.9 %all-gather.5.cloned.1.call-done = bf16[8192,256]{1,0:T(8,128)(2,1)} async-done(((bf16[2048,256]{1,0:T(8,128)(2,1)}), bf16[8192,256]{1,0:T(8,128)(2,1)}) %all-gather.5.cloned.1.call-update) | async-done | bytes 4194320 | tf_op jit(solution)/shard_map/all_gather | solution.py:43
  111.8 3.3 multiply_reduce_fusion.1
  115.9 11.4 %gather_fusion.11 = bf16[256,128,256]{2,1,0:T(8,128)(2,1)} fusion(bf16[64,128,256]{2,1,0:T(8,128)(2,1)} %bitcast.123, s32[1024]{0:T(1024)S(1)} %pad_clamp_fusion.1), kind=kCustom, calls=%fused_computation.11 | custom fusion | bytes 33555456 | tf_op jit(solution)/shard_map/gather | solution.py:62
  127.3 97.7 %all-gather.7.cloned.1.call-done = bf16[56,256,256]{2,1,0:T(8,128)(2,1)} async-done(((bf16[7,256,256]{2,1,0:T(8,128)(2,1)}), bf16[56,256,256]{2,1,0:T(8,128)(2,1)}) %all-gather.7.cloned.1.call-update) | async-done | bytes 7340048 | tf_op jit(solution)/shard_map/all_gather | solution.py:52
  225.0 5.0 %multiply_reduce_fusion = f32[56,256]{1,0:T(8,128)S(1)} fusion(bf16[56,256,256]{2,1,0:T(8,128)(2,1)} %all-gather.7.cloned.1.call-done), kind=kLoop, calls=%fused_computation.18 | loop fusion | flops 10995712 | bytes 7397376 | tf_op jit(solution)/shard_map/reduce_sum | solution.py:18
  232.1 8.7 %gather_fusion.5 = bf16[64,256,256]{2,1,0:T(8,128)(2,1)} fusion(bf16[56,256,256]{2,1,0:T(8,128)(2,1)} %all-gather.7.cloned.1.call-done, s32[1024]{0:T(1024)S(1)} %get-tuple-element.12), kind=kCustom, calls=%fused_computation.5 | custom fusion | bytes 16777472 | tf_op jit(solution)/shard_map/gather | solution.py:82
  240.8 7.4 %fusion.24 = f32[64,128,64]{1,2,0:T(8,128)} fusion(bf16[64,256,64]{1,2,0:T(8,128)(2,1)S(1)} %copy-done.5, f32[64,256]{1,0:T(8,128)S(1)} %gather_fusion.4, f32[64,128]{1,0:T(8,128)S(1)} %bitcast.130, pred[64]{0:T(512)(128)(4,1)S(1)} %get-tuple-element.7, bf16[64,256,256]{2,1,0:T(8,128)(2,1)} %gather_fusion.5, bf16[64,128,256]{2,1,0:T(8,128)(2,1)} %bitcast.124), kind=kOutput, calls=%fused_computation.40 | convolution fusion | flops 1354760192 | bytes 16875584 | tf_op jit(solution)/shard_map/bis,bsw->biw/dot_general | solution.py:30
  248.2 8.7 %gather_fusion.2 = bf16[64,256,256]{2,1,0:T(8,128)(2,1)} fusion(bf16[56,256,256]{2,1,0:T(8,128)(2,1)} %all-gather.7.cloned.1.call-done, s32[1024]{0:T(1024)S(1)} %pad_clamp_fusion.4), kind=kCustom, calls=%fused_computation.2 | custom fusion | bytes 16777472 | tf_op jit(solution)/shard_map/gather | solution.py:82
  256.9 7.4 %fusion.22 = f32[64,128,64]{1,2,0:T(8,128)} fusion(bf16[64,256,64]{1,2,0:T(8,128)(2,1)S(1)} %copy-done.4, f32[64,256]{1,0:T(8,128)S(1)} %gather_fusion.1, f32[64,128]{1,0:T(8,128)S(1)} %bitcast.131, pred[64]{0:T(512)(128)(4,1)S(1)} %get-tuple-element.6, bf16[64,256,256]{2,1,0:T(8,128)(2,1)} %gather_fusion.2, bf16[64,128,256]{2,1,0:T(8,128)(2,1)} %bitcast.125), kind=kOutput, calls=%fused_computation.39 | convolution fusion | flops 1354760192 | bytes 16875584 | tf_op jit(solution)/shard_map/bis,bsw->biw/dot_general | solution.py:30
  264.4 8.9 %gather_fusion.8 = bf16[64,256,256]{2,1,0:T(8,128)(2,1)} fusion(bf16[56,256,256]{2,1,0:T(8,128)(2,1)} %all-gather.7.cloned.1.call-done, s32[1024]{0:T(1024)S(1)} %get-tuple-element.11), kind=kCustom, calls=%fused_computation.8 | custom fusion | bytes 16777472 | tf_op jit(solution)/shard_map/gather | solution.py:82
  273.3 8.9 %add_bitcast_fusion = f32[64,8,8,128]{3,2,1,0:T(8,128)} fusion(f32[64,128,64]{1,2,0:T(8,128)} %fusion.22, f32[64,128,64]{1,2,0:T(8,128)} %fusion.24, bf16[64,256,64]{1,2,0:T(8,128)(2,1)S(1)} %copy-done.3, f32[64,256]{1,0:T(8,128)S(1)} %gather_fusion.7, f32[64,128]{1,0:T(8,128)S(1)} %bitcast.132, pred[64]{0:T(512)(128)(4,1)S(1)} %get-tuple-element.5, ...), kind=kOutput, calls=%fused_computation.49 | convolution fusion | flops 1355808768 | bytes 21069888 | tf_op jit(solution)/shard_map/bis,bsw->biw/dot_general | solution.py:30
  282.2 3.1 copy.47
  285.3 12.0 %fusion.84 = bf16[16,128,2048]{1,2,0:T(8,128)(2,1)S(1)} fusion(f32[16,2048]{1,0:T(8,128)S(1)} %add.258, f32[16,128]{1,0:T(8,128)S(1)} %constant_dynamic-slice_fusion, pred[16,2048]{1,0:T(8,128)(4,1)S(1)} %bitcast.137, bf16[16,2048,256]{2,1,0:T(8,128)(2,1)} %bitcast.133, bf16[16,128,256]{2,1,0:T(8,128)(2,1)S(1)} %bitcast.127), kind=kOutput, calls=%fused_computation.17.clone.clone.clone.clone.1 | convolution fusion | flops 2172649472 | bytes 26386432 | tf_op jit(solution)/shard_map/bie,bse->bis/dot_general | solution.py:22
  297.3 5.0 %fusion.39 = f32[16,8,8,128]{3,2,1,0:T(8,128)S(1)} fusion(bf16[16,2048,64]{1,0,2:T(8,128)(2,1)S(1)} %copy-done.2, bf16[16,128,2048]{1,2,0:T(8,128)(2,1)S(1)} %fusion.84), kind=kOutput, calls=%fused_computation.50 | convolution fusion | flops 536870912 | bytes 13107200 | tf_op jit(solution)/shard_map/bis,bsw->biw/dot_general | solution.py:30
  302.3 33.1 %all-reduce.2.cloned.1.call-done = f32[8192,64]{0,1:T(8,128)} async-done(((f32[8192,64]{0,1:T(8,128)}), f32[8192,64]{0,1:T(8,128)}) %all-reduce.2.cloned.1.call-update) | async-done | bytes 2097168 | tf_op jit(solution)/shard_map/psum | solution.py:87
  (51 shorter events, 10.7 us)
Async XLA Ops:
  6.5 8.6 %copy-start.7 = (s32[7,256]{1,0:T(8,128)S(1)}, s32[7,256]{1,0:T(8,128)}, u32[]{:S(2)}) copy-start(s32[7,256]{1,0:T(8,128)} %param.10) | copy-start | bytes 21508
  6.5 9.9 %copy-start.6 = (s32[16,16]{1,0:T(8,128)S(1)}, s32[16,16]{1,0:T(8,128)}, u32[]{:S(2)}) copy-start(s32[16,16]{1,0:T(8,128)} %param.8) | copy-start | bytes 3076
  6.5 10.1 %copy-start.8 = (s32[64,3,1]{0,2,1:T(1,128)S(1)}, s32[64,3,1]{0,2,1:T(1,128)}, u32[]{:S(2)}) copy-start(s32[64,3,1]{0,2,1:T(1,128)} %param.9) | copy-start | bytes 2308
  6.5 21.7 %all-gather.11.cloned.1.call-start = ((), (), s32[]{:S(2)}) async-start(), calls=%async_computation.4 | async-start | bytes 1310720 | tf_op jit(solution)/shard_map/all_gather | solution.py:44
  7.3 68.0 %all-gather.9.cloned.1.call-start = ((), (), s32[]{:S(2)}) async-start(), calls=%async_computation.2 | async-start | bytes 2064384 | tf_op jit(solution)/shard_map/all_gather | solution.py:53
  8.0 103.8 %all-gather.5.cloned.1.call-start = ((), (), s32[]{:S(2)}) async-start(), calls=%async_computation | async-start | bytes 5242880 | tf_op jit(solution)/shard_map/all_gather | solution.py:43
  8.7 216.3 %all-gather.7.cloned.1.call-start = ((), (), s32[]{:S(2)}) async-start(), calls=%async_computation.1 | async-start | bytes 8257536 | tf_op jit(solution)/shard_map/all_gather | solution.py:52
  16.4 319.0 %all-reduce.2.cloned.1.call-start = ((), (), s32[]{:S(2)}) async-start(), calls=%async_computation.3 | async-start | bytes 4194304 | tf_op jit(solution)/shard_map/psum | solution.py:87
  75.2 3.6 %copy-start = (bf16[56,256,64]{1,2,0:T(8,128)(2,1)S(1)}, bf16[56,256,64]{1,2,0:T(8,128)(2,1)}, u32[]{:S(2)}) copy-start(bf16[56,256,64]{1,2,0:T(8,128)(2,1)} %all-gather.9.cloned.1.call-done) | copy-start | bytes 5505028
  232.1 8.8 %copy-start.5 = (bf16[64,256,64]{1,2,0:T(8,128)(2,1)S(1)}, bf16[64,256,64]{1,2,0:T(8,128)(2,1)}, u32[]{:S(2)}) copy-start(bf16[64,256,64]{1,2,0:T(8,128)(2,1)} %gather_fusion.6) | copy-start | bytes 6291460
  248.2 8.7 %copy-start.4 = (bf16[64,256,64]{1,2,0:T(8,128)(2,1)S(1)}, bf16[64,256,64]{1,2,0:T(8,128)(2,1)}, u32[]{:S(2)}) copy-start(bf16[64,256,64]{1,2,0:T(8,128)(2,1)} %gather_fusion.3) | copy-start | bytes 6291460
  264.4 8.9 %copy-start.3 = (bf16[64,256,64]{1,2,0:T(8,128)(2,1)S(1)}, bf16[64,256,64]{1,2,0:T(8,128)(2,1)}, u32[]{:S(2)}) copy-start(bf16[64,256,64]{1,2,0:T(8,128)(2,1)} %gather_fusion.9) | copy-start | bytes 6291460
  273.3 12.0 %copy-start.1 = (bf16[2048,256]{1,0:T(8,128)(2,1)S(1)}, bf16[2048,256]{1,0:T(8,128)(2,1)}, u32[]{:S(2)}) copy-start(bf16[2048,256]{1,0:T(8,128)(2,1)} %param.6) | copy-start | bytes 3145732
  285.3 12.0 %copy-start.2 = (bf16[16,2048,64]{1,0,2:T(8,128)(2,1)S(1)}, bf16[16,2048,64]{1,0,2:T(8,128)(2,1)}, u32[]{:S(2)}) copy-start(bf16[16,2048,64]{1,0,2:T(8,128)(2,1)} %reshape.319) | copy-start | bytes 12582916
Sparse Core Ops, SparseCore 0:
  8.9 19.2 all-gather.10
  30.4 44.7 all-gather.8
  76.8 34.9 all-gather.4
  113.8 111.1 all-gather.6
  285.4 49.9 all-reduce.1
where the time goes:
time: 345 us; the launch traced here: 344 us
  waiting for transfers between devices  202 us (59%)
  local copies, waits for them, and re-layouts  76.5 us (22%)
  matrix products  40.7 us (12%)
  between operations  13.3 us (4%)
  other arithmetic  11.6 us (3%)
    all_gather x1, waiting for transfers between devices, shards(): lax.all_gather(skel_pts, 'tgt', axis=0, tiled=True)  97.7 us
    psum x1, waiting for transfers between devices, shards(): whole_term = lax.psum(far_total.reshape(row_count, WCOL), 'src')  33.1 us
    all_gather x1, waiting for transfers between devices, shards(): lax.all_gather(points, 'src', axis=0, tiled=True)  28.9 us
    dot_general x4, matrix products, apply_tile(): jnp.einsum('bis,bsw->biw', kernel, source_weights, preferred_element_type...  28.7 us
    all_gather x1, waiting for transfers between devices, shards(): lax.all_gather(equiv_weights, 'tgt', axis=0, tiled=True)  28.3 us
    gather x3, local copies, waits for them, and re-layouts, shards(): panel_pts[panel_rows]  26.4 us
    dot_general x1, matrix products, tile_kernel(): jnp.einsum('bie,bse->bis', targets, sources, preferred_element_type=jnp.f...  12 us
    all_gather x1, waiting for transfers between devices, shards(): lax.all_gather(weights, 'src', axis=0, tiled=True)  11.4 us
  transfers between devices with their start and end apart: 5, of which 5 were waited for; matrix products, arithmetic and copies ran while one was open for 19% of the time, Pallas kernels for 0%

commit v1 on v0

v1 whole, which is shorter than its diff:
```python
import functools

import jax
import jax.numpy as jnp
from jax import lax
from jax.experimental import pallas as pl
from jax.experimental.pallas import tpu as pltpu
from jax.sharding import PartitionSpec as P

E = 256
WCOL = 64
BLK = 128
RANK = 256
NEAR = 16
LEVELS = 3
Z = 4

BROWS = BLK + BLK // 4
NROWS = RANK + RANK // 4
MESH = pl.DeviceIdType.MESH


def pack(w):
    q = w.shape[0] // 4
    return jnp.concatenate([w[k * q : (k + 1) * q, :] for k in range(4)], axis=1)


def unpack(p):
    return jnp.concatenate([p[:, k * WCOL : (k + 1) * WCOL] for k in range(4)], axis=0)


def row_norms(x):
    sq = jnp.square(x.astype(jnp.float32))
    hi = sq.astype(jnp.bfloat16)
    lo = (sq - hi.astype(jnp.float32)).astype(jnp.bfloat16)
    twos = jnp.full((16, E), 2.0, jnp.bfloat16)
    dims = (((1,), (1,)), ((), ()))
    total = lax.dot_general(twos, hi, dims, preferred_element_type=jnp.float32)
    total = total + lax.dot_general(twos, lo, dims, preferred_element_type=jnp.float32)
    return total[0:1, :]


def targets_of(x):
    sq = jnp.square(x.astype(jnp.float32))
    return x * jnp.bfloat16(4.0), 2.0 * jnp.sum(sq, axis=1, keepdims=True)


def tile(xt, tn, src, sn, w):
    d = lax.dot_general(xt, src, (((1,), (1,)), ((), ())), preferred_element_type=jnp.float32)
    k = jnp.exp((d - tn) - sn).astype(jnp.bfloat16)
    return jnp.dot(k, w, preferred_element_type=jnp.float32)


def kernel(
    n_tgt, n_src, blk_dev, level_nodes,
    pts, wts, skel, ew, near, far, out,
    grp, gn, l0, l1, l2, n0, n1, n2, facc, red_out, red_in,
    gs, gr, zs, zr, xs, xr, rs, rr,
):
    X = n_tgt // Z
    tgt, src = lax.axis_index("tgt"), lax.axis_index("src")
    z, x = tgt // X, tgt % X
    levels, norms = (l0, l1, l2), (n0, n1, n2)
    pairs = blk_dev // 2

    def z_peer(k):
        return lax.rem(z + k, Z) * X + x

    def x_peer(k):
        return z * X + lax.rem(x + k, X)

    def s_peer(k):
        return lax.rem(src + k, n_src)

    barrier = pltpu.get_barrier_semaphore()
    for k in range(1, Z):
        pl.semaphore_signal(barrier, inc=1, device_id=(z_peer(k), src), device_id_type=MESH)
    for k in range(1, X):
        pl.semaphore_signal(barrier, inc=1, device_id=(x_peer(k), src), device_id_type=MESH)
    for k in range(1, n_src):
        pl.semaphore_signal(barrier, inc=1, device_id=(tgt, s_peer(k)), device_id_type=MESH)

    def z_copy(l, k):
        own = levels[l].at[pl.ds(tgt * level_nodes[l], level_nodes[l])]
        return pltpu.make_async_remote_copy(
            own, own, zs.at[l * Z + k], zr.at[l * Z + k], (z_peer(k), src), MESH
        )

    def shard_of(k):
        return lax.rem(z - k + Z, Z) * X + x

    def x_copy(l, k, j):
        held = levels[l].at[pl.ds(shard_of(k) * level_nodes[l], level_nodes[l])]
        i = (l * Z + k) * X + j
        return pltpu.make_async_remote_copy(held, held, xs.at[i], xr.at[i], (x_peer(j), src), MESH)

    def g_copy(k):
        own = grp.at[pl.ds(src * blk_dev, blk_dev)]
        return pltpu.make_async_remote_copy(own, own, gs.at[k], gr.at[k], (tgt, s_peer(k)), MESH)

    def r_copy(k):
        return pltpu.make_async_remote_copy(
            red_out.at[k], red_in.at[k], rs.at[k], rr.at[k], (tgt, s_peer(k)), MESH
        )

    def gather_level(l):
        size = 4 * BLK * 2**l
        start = sum(level_nodes[:l])
        for r in range(level_nodes[l]):
            node = start + r
            acc = jnp.zeros((RANK, E), jnp.float32)
            for c in range(size // 512):
                base = r * size + c * 512
                pick = lax.broadcasted_iota(jnp.int32, (RANK, 512), 1) == skel[:, node : node + 1] - base
                pick = jnp.where(pick, 1.0, 0.0).astype(jnp.bfloat16)
                acc = acc + jnp.dot(pick, pts[base : base + 512, :], preferred_element_type=jnp.float32)
            at = tgt * level_nodes[l] + r
            levels[l][at, 0:RANK, :] = acc.astype(jnp.bfloat16)
            levels[l][at, RANK:NROWS, :] = pack(ew[node])

    def level_norms(l, shard):
        def body(r, c):
            at = shard * level_nodes[l] + r
            norms[l][at] = row_norms(levels[l][at, 0:RANK, :])
            return c
        lax.fori_loop(0, level_nodes[l], body, 0)

    gather_level(2)
    pl.semaphore_wait(barrier, (Z - 1) + (X - 1) + (n_src - 1))

    def send_level(l):
        for k in range(1, Z):
            z_copy(l, k).start()
        for j in range(1, X):
            x_copy(l, 0, j).start()

    send_level(2)
    gather_level(1)
    send_level(1)
    gather_level(0)
    send_level(0)

    def pack_block(b, c):
        at = src * blk_dev + b
        grp[at, 0:BLK, :] = pts[pl.ds(pl.multiple_of(b * BLK, BLK), BLK), :]
        grp[at, BLK:BROWS, :] = pack(wts[pl.ds(pl.multiple_of(b * BLK, BLK), BLK), :])
        return c

    lax.fori_loop(0, blk_dev, pack_block, 0)
    for k in range(1, n_src):
        g_copy(k).start()

    def forward(l, k):
        z_copy(l, k).wait_recv()
        for j in range(1, X):
            x_copy(l, k, j).start()

    def finish(l):
        for k in range(Z):
            for j in range(1, X):
                x_copy(l, k, j).wait_recv()
                level_norms(l, lax.rem(z - k + Z, Z) * X + lax.rem(x - j + X, X))

    for l in (2, 1, 0):
        level_norms(l, tgt)
    for l in (2, 1):
        for k in range(1, Z):
            forward(l, k)
            level_norms(l, shard_of(k))

    for k in range(1, n_src):
        g_copy(k).wait_recv()

    def group_norms(b, c):
        gn[b] = row_norms(grp[b, 0:BLK, :])
        return c

    lax.fori_loop(0, n_src * blk_dev, group_norms, 0)

    def far_block(l, b):
        xt, tn = targets_of(grp[b, 0:BLK, :])
        e = far[l, b]
        i = jnp.maximum(e, 0)
        sn = norms[l][i] + jnp.where(e >= 0, 0.0, 1e30)
        return tile(xt, tn, levels[l][i, 0:RANK, :], sn, unpack(levels[l][i, RANK:NROWS, :]))

    def far_pair(l, p):
        return jnp.concatenate([far_block(l, 2 * p), far_block(l, 2 * p + 1)], axis=1)

    def near_block(b, c):
        rows = pl.ds(pl.multiple_of(b * BLK, BLK), BLK)
        xt, tn = targets_of(pts[rows, :])
        acc = jnp.zeros((BLK, WCOL), jnp.float32)
        for s in range(0, NEAR, 2):
            e0, e1 = near[b, s], near[b, s + 1]
            i0, i1 = jnp.maximum(e0, 0), jnp.maximum(e1, 0)
            sources = jnp.concatenate([grp[i0, 0:BLK, :], grp[i1, 0:BLK, :]], axis=0)
            sn = jnp.concatenate(
                [
                    gn[i0] + jnp.where(e0 >= 0, 0.0, 1e30),
                    gn[i1] + jnp.where(e1 >= 0, 0.0, 1e30),
                ],
                axis=1,
            )
            w = jnp.concatenate([unpack(grp[i0, BLK:BROWS, :]), unpack(grp[i1, BLK:BROWS, :])], axis=0)
            acc = acc + tile(xt, tn, sources, sn, w)
        out[rows, :] = acc
        return c

    half = blk_dev // 2
    lax.fori_loop(0, half, near_block, 0)
    forward(0, 1)
    level_norms(0, shard_of(1))
    lax.fori_loop(half, blk_dev, near_block, 0)
    forward(0, 2)
    level_norms(0, shard_of(2))
    finish(2)

    def far2(p, c):
        facc[p] = far_pair(2, p)
        return c

    def far1(p, c):
        facc[p] = facc[p] + far_pair(1, p)
        return c

    lax.fori_loop(0, n_src * pairs, far2, 0)
    forward(0, 3)
    level_norms(0, shard_of(3))
    finish(1)
    lax.fori_loop(0, n_src * pairs, far1, 0)
    finish(0)

    for j in range(1, n_src):
        def far0(p, c, j=j):
            at = s_peer(j) * pairs + p
            red_out[j, p] = (facc[at] + far_pair(0, at)).astype(jnp.bfloat16)
            return c

        lax.fori_loop(0, pairs, far0, 0)
        r_copy(j).start()

    def far_own(p, c):
        at = src * pairs + p
        facc[at] = facc[at] + far_pair(0, at)
        return c

    lax.fori_loop(0, pairs, far_own, 0)
    for j in range(1, n_src):
        r_copy(j).wait_recv()

    def last(p, c):
        total = facc[src * pairs + p]
        for j in range(1, n_src):
            total = total + red_in[j, p].astype(jnp.float32)
        for h in range(2):
            rows = pl.ds(pl.multiple_of((2 * p + h) * BLK, BLK), BLK)
            out[rows, :] = out[rows, :] + total[:, h * WCOL : (h + 1) * WCOL]
        return c

    lax.fori_loop(0, pairs, last, 0)

    for l in (2, 1, 0):
        for k in range(1, Z):
            z_copy(l, k).wait_send()
        for k in range(Z):
            for j in range(1, X):
                x_copy(l, k, j).wait_send()
    for k in range(1, n_src):
        g_copy(k).wait_send()
        r_copy(k).wait_send()


def shards(n_tgt, n_src, points, weights, near_list, far_list, skel_index, equiv_weights):
    point_dev = points.shape[0]
    blk_dev = point_dev // BLK
    level_nodes = [blk_dev // (4 * 2**l) for l in range(LEVELS)]
    group = n_src * blk_dev
    X = n_tgt // Z
    vmem, smem = pl.BlockSpec(memory_space=pltpu.VMEM), pl.BlockSpec(memory_space=pltpu.SMEM)
    bf16, f32 = jnp.bfloat16, jnp.float32
    dma = pltpu.SemaphoreType.DMA
    return pl.pallas_call(
        functools.partial(kernel, n_tgt, n_src, blk_dev, level_nodes),
        out_shape=jax.ShapeDtypeStruct((point_dev, WCOL), f32),
        in_specs=[vmem, vmem, vmem, vmem, smem, smem],
        out_specs=vmem,
        scratch_shapes=[
            pltpu.VMEM((group, BROWS, E), bf16),
            pltpu.VMEM((group, 1, BLK), f32),
            *[pltpu.VMEM((n_tgt * n, NROWS, E), bf16) for n in level_nodes],
            *[pltpu.VMEM((n_tgt * n, 1, RANK), f32) for n in level_nodes],
            pltpu.VMEM((group // 2, BLK, 2 * WCOL), f32),
            pltpu.VMEM((n_src, blk_dev // 2, BLK, 2 * WCOL), bf16),
            pltpu.VMEM((n_src, blk_dev // 2, BLK, 2 * WCOL), bf16),
            dma((n_src,)), dma((n_src,)),
            dma((LEVELS * Z,)), dma((LEVELS * Z,)),
            dma((LEVELS * Z * X,)), dma((LEVELS * Z * X,)),
            dma((n_src,)), dma((n_src,)),
        ],
        compiler_params=pltpu.CompilerParams(
            collective_id=0, has_side_effects=True, vmem_limit_bytes=56 * 2**20
        ),
    )(
        points, weights, skel_index.T, equiv_weights, near_list, far_list[:, :, 0].T,
    )


def solution(mesh):
    in_specs = (
        P(("tgt", "src"), None),
        P(("tgt", "src"), None),
        P(("tgt", "src"), None),
        P("tgt", None, "src"),
        P(("tgt", "src"), None),
        P(("tgt", "src"), None, None),
    )
    out_specs = P(("tgt", "src"), None)
    body = functools.partial(shards, mesh.shape["tgt"], mesh.shape["src"])
    return jax.shard_map(body, mesh=mesh, in_specs=in_specs, out_specs=out_specs, check_vma=False)
```

time: 345 us -> 191 us (0.55)
  the two profiles are of different devices: /device:TPU:1 before, /device:TPU:9 now
where the time goes in v1:
time: 191 us
  Pallas kernels  183 us (96%)
  local copies, waits for them, and re-layouts  8.08 us (4%)
    pallas_call x1, Pallas kernels, shards(): pl.pallas_call(functools.partial(kernel, n_tgt, n_src, blk_dev, level_nod...  183 us
    unnamed x6, local copies, waits for them, and re-layouts  5.75 us

profile of v1, /device:TPU:9, one launch (start us, length us, event | category | flops | bytes accessed | tf_op | source)
XLA Modules:
  0.0 190.7 jit_solution(16105139813162006656)
XLA Ops:
  0.0 1.3 copy.13
  1.3 1.5 copy.7
  2.8 0.0 copy-start
  2.8 2.0 %copy.9.ew = bf16[7,256,64]{2,1,0:T(8,128)(2,1)} copy(bf16[7,256,64]{1,2,0:T(8,128)(2,1)} %param.11) | data formatting | bytes 458752 | tf_op args[5]
  4.7 0.0 copy-done
  4.7 1.0 copy.8.wts
  5.7 182.6 %shard_map.64 = f32[2048,64]{1,0:T(8,128)} custom-call(bf16[2048,256]{1,0:T(8,128)(2,1)} %pts.1, bf16[2048,64]{1,0:T(8,128)(2,1)} %copy.8.wts, s32[256,7]{1,0:T(8,128)} %bitcast.6, bf16[7,256,64]{2,1,0:T(8,128)(2,1)} %copy.9.ew, s32[16,16]{1,0:T(8,128)} %near.1, s32[3,64]{1,0:T(4,128)} %bitcast.7), custom_call_target="tpu_custom_call" | custom-call | tf_op jit(solution)/shard_map/pallas_call | solution.py:283
  188.3 2.3 %copy.10 = f32[2048,64]{0,1:T(8,128)} copy(f32[2048,64]{1,0:T(8,128)} %shard_map.64) | data formatting | bytes 1048576 | tf_op jit(solution)/shard_map/pallas_call | solution.py:283
Async XLA Ops:
  2.8 2.0 %copy-start = (bf16[2048,64]{0,1:T(8,128)(2,1)S(1)}, bf16[2048,64]{0,1:T(8,128)(2,1)}, u32[]{:S(2)}) copy-start(bf16[2048,64]{0,1:T(8,128)(2,1)} %param.7) | copy-start | bytes 786436

commit v2 on v1

--- a/solution.py
+++ b/solution.py
@@ -58,49 +58,79 @@
     gs, gr, zs, zr, xs, xr, rs, rr,
 ):
     X = n_tgt // Z
+    Y = n_src // 2
     tgt, src = lax.axis_index("tgt"), lax.axis_index("src")
     z, x = tgt // X, tgt % X
+    y, core = src // 2, src % 2
     levels, norms = (l0, l1, l2), (n0, n1, n2)
     pairs = blk_dev // 2
-
-    def z_peer(k):
-        return lax.rem(z + k, Z) * X + x
-
-    def x_peer(k):
-        return z * X + lax.rem(x + k, X)
-
-    def s_peer(k):
-        return lax.rem(src + k, n_src)
+    half0 = level_nodes[0] // 2
+    items = ((2, 0, level_nodes[2]), (1, 0, level_nodes[1]), (0, 0, half0), (0, half0, half0))
+    mates = [(dy, dc) for dy in range(1, Y) for dc in range(2)] + [(0, 1)]
+
+    def x_peer(j):
+        return z * X + lax.rem(x + j, X)
+
+    def x_from(j):
+        return lax.rem(x - j + X, X)
+
+    def s_peer(dy, dc):
+        return lax.rem(y + dy, Y) * 2 + (1 - core if dc else core)
 
     barrier = pltpu.get_barrier_semaphore()
-    for k in range(1, Z):
-        pl.semaphore_signal(barrier, inc=1, device_id=(z_peer(k), src), device_id_type=MESH)
-    for k in range(1, X):
-        pl.semaphore_signal(barrier, inc=1, device_id=(x_peer(k), src), device_id_type=MESH)
-    for k in range(1, n_src):
-        pl.semaphore_signal(barrier, inc=1, device_id=(tgt, s_peer(k)), device_id_type=MESH)
-
-    def z_copy(l, k):
-        own = levels[l].at[pl.ds(tgt * level_nodes[l], level_nodes[l])]
+
+    def greet(t, s):
+        pl.semaphore_signal(barrier, inc=1, device_id=(t, s), device_id_type=MESH)
+
+    @pl.when(z > 0)
+    def _():
+        greet(tgt - X, src)
+
+    @pl.when(z < Z - 1)
+    def _():
+        greet(tgt + X, src)
+
+    for j in range(1, X):
+        greet(x_peer(j), src)
+    for dy, dc in mates:
+        greet(tgt, s_peer(dy, dc))
+
+    def nodes(i, owner):
+        l, first, count = items[i]
+        return levels[l].at[pl.ds(owner * level_nodes[l] + first, count)]
+
+    def z_copy(i, d, k, col, j):
+        held = nodes(i, (z - d * k) * X + col)
+        at = ((i * 2 + (d + 1) // 2) * Z + k) * X + j
         return pltpu.make_async_remote_copy(
-            own, own, zs.at[l * Z + k], zr.at[l * Z + k], (z_peer(k), src), MESH
+            held, held, zs.at[at], zr.at[at], (tgt + d * X, src), MESH
         )
 
-    def shard_of(k):
-        return lax.rem(z - k + Z, Z) * X + x
-
-    def x_copy(l, k, j):
-        held = levels[l].at[pl.ds(shard_of(k) * level_nodes[l], level_nodes[l])]
-        i = (l * Z + k) * X + j
-        return pltpu.make_async_remote_copy(held, held, xs.at[i], xr.at[i], (x_peer(j), src), MESH)
+    def x_copy(i, d, k, j):
+        held = nodes(i, (z - d * k) * X + x)
+        at = ((i * 2 + (d + 1) // 2) * Z + k) * X + j
+        return pltpu.make_async_remote_copy(held, held, xs.at[at], xr.at[at], (x_peer(j), src), MESH)
+
+    def has(d, k):
+        return (z >= k) if d > 0 else (z + k <= Z - 1)
+
+    def more(d):
+        return (z < Z - 1) if d > 0 else (z > 0)
 
     def g_copy(k):
         own = grp.at[pl.ds(src * blk_dev, blk_dev)]
-        return pltpu.make_async_remote_copy(own, own, gs.at[k], gr.at[k], (tgt, s_peer(k)), MESH)
-
-    def r_copy(k):
+        return pltpu.make_async_remote_copy(own, own, gs.at[k], gr.at[k], (tgt, s_peer(k, 0)), MESH)
+
+    def c_copy(k):
+        row = (lax.rem(y - k + Y, Y) * 2 + core) * blk_dev
+        held = grp.at[pl.ds(row, blk_dev)]
         return pltpu.make_async_remote_copy(
-            red_out.at[k], red_in.at[k], rs.at[k], rr.at[k], (tgt, s_peer(k)), MESH
+            held, held, gs.at[Y + k], gr.at[Y + k], (tgt, s_peer(0, 1)), MESH
+        )
+
+    def r_copy(m):
+        return pltpu.make_async_remote_copy(
+            red_out.at[m], red_in.at[m], rs.at[m], rr.at[m], (tgt, s_peer(*mates[m])), MESH
         )
 
     def gather_level(l):
@@ -118,27 +148,67 @@
             levels[l][at, 0:RANK, :] = acc.astype(jnp.bfloat16)
             levels[l][at, RANK:NROWS, :] = pack(ew[node])
 
-    def level_norms(l, shard):
-        def body(r, c):
-            at = shard * level_nodes[l] + r
+    def item_norms(i, owner):
+        l, first, count = items[i]
+        for r in range(count):
+            at = owner * level_nodes[l] + first + r
             norms[l][at] = row_norms(levels[l][at, 0:RANK, :])
-            return c
-        lax.fori_loop(0, level_nodes[l], body, 0)
+
+    def send_own(i):
+        for d in (1, -1):
+            @pl.when(more(d))
+            def _(d=d):
+                z_copy(i, d, 0, x, 0).start()
+        for j in range(1, X):
+            x_copy(i, 1, 0, j).start()
+
+    def forward(i, d, k, norm=True):
+        @pl.when(has(d, k))
+        def _():
+            z_copy(i, d, k - 1, x, 0).wait_recv()
+            if k < Z - 1:
+                @pl.when(more(d))
+                def _():
+                    z_copy(i, d, k, x, 0).start()
+            if i > 0:
+                for j in range(1, X):
+                    x_copy(i, d, k, j).start()
+            if norm:
+                item_norms(i, (z - d * k) * X + x)
+
+    def forward_other(d, k):
+        @pl.when(has(d, k))
+        def _():
+            for j in range(1, X):
+                z_copy(0, d, k - 1, x_from(j), j).wait_recv()
+                if k < Z - 1:
+                    @pl.when(more(d))
+                    def _(j=j):
+                        z_copy(0, d, k, x_from(j), j).start()
+                item_norms(0, (z - d * k) * X + x_from(j))
+
+    def crossed(i, d, k):
+        @pl.when(has(d, k))
+        def _():
+            for j in range(1, X):
+                x_copy(i, d, k, j).wait_recv()
+                item_norms(i, (z - d * k) * X + x_from(j))
 
     gather_level(2)
-    pl.semaphore_wait(barrier, (Z - 1) + (X - 1) + (n_src - 1))
-
-    def send_level(l):
-        for k in range(1, Z):
-            z_copy(l, k).start()
-        for j in range(1, X):
-            x_copy(l, 0, j).start()
-
-    send_level(2)
+    pl.semaphore_wait(
+        barrier, (z > 0).astype(jnp.int32) + (z < Z - 1).astype(jnp.int32) + (X - 1) + len(mates)
+    )
+    send_own(0)
     gather_level(1)
-    send_level(1)
+    send_own(1)
+    for j in range(1, X):
+        x_copy(0, 1, 0, j).wait_recv()
+        for d in (1, -1):
+            @pl.when(more(d))
+            def _(d=d, j=j):
+                z_copy(0, d, 0, x_from(j), j).start()
     gather_level(0)
-    send_level(0)
+    send_own(2)
 
     def pack_block(b, c):
         at = src * blk_dev + b
@@ -147,35 +217,35 @@
         return c
 
     lax.fori_loop(0, blk_dev, pack_block, 0)
-    for k in range(1, n_src):
+    for k in range(1, Y):
         g_copy(k).start()
-
-    def forward(l, k):
-        z_copy(l, k).wait_recv()
-        for j in range(1, X):
-            x_copy(l, k, j).start()
-
-    def finish(l):
-        for k in range(Z):
-            for j in range(1, X):
-                x_copy(l, k, j).wait_recv()
-                level_norms(l, lax.rem(z - k + Z, Z) * X + lax.rem(x - j + X, X))
-
-    for l in (2, 1, 0):
-        level_norms(l, tgt)
-    for l in (2, 1):
-        for k in range(1, Z):
-            forward(l, k)
-            level_norms(l, shard_of(k))
-
-    for k in range(1, n_src):
-        g_copy(k).wait_recv()
+    c_copy(0).start()
+    for i in range(4):
+        item_norms(i, tgt)
+    for j in range(1, X):
+        item_norms(0, z * X + x_from(j))
+
+    ways = [(d, k) for k in range(1, Z) for d in (1, -1)]
+    for k in range(1, Z):
+        for d in (1, -1):
+            forward(0, d, k)
+            forward(1, d, k)
+        for d in (1, -1):
+            forward_other(d, k)
+        if k == 1:
+            send_own(3)
+            for j in range(1, Y):
+                g_copy(j).wait_recv()
+                c_copy(j).start()
+
+    for k in range(Y):
+        c_copy(k).wait_recv()
 
     def group_norms(b, c):
         gn[b] = row_norms(grp[b, 0:BLK, :])
         return c
 
-    lax.fori_loop(0, n_src * blk_dev, group_norms, 0)
+    lax.fori_loop(0, n_src * blk_dev, group_norms, 0, unroll=4)
 
     def far_block(l, b):
         xt, tn = targets_of(grp[b, 0:BLK, :])
@@ -207,15 +277,6 @@
         out[rows, :] = acc
         return c
 
-    half = blk_dev // 2
-    lax.fori_loop(0, half, near_block, 0)
-    forward(0, 1)
-    level_norms(0, shard_of(1))
-    lax.fori_loop(half, blk_dev, near_block, 0)
-    forward(0, 2)
-    level_norms(0, shard_of(2))
-    finish(2)
-
     def far2(p, c):
         facc[p] = far_pair(2, p)
         return c
@@ -224,35 +285,57 @@
         facc[p] = facc[p] + far_pair(1, p)
         return c
 
-    lax.fori_loop(0, n_src * pairs, far2, 0)
-    forward(0, 3)
-    level_norms(0, shard_of(3))
-    finish(1)
-    lax.fori_loop(0, n_src * pairs, far1, 0)
-    finish(0)
-
-    for j in range(1, n_src):
-        def far0(p, c, j=j):
-            at = s_peer(j) * pairs + p
-            red_out[j, p] = (facc[at] + far_pair(0, at)).astype(jnp.bfloat16)
+    count = n_src * pairs
+    forward(2, 1, 1)
+    forward(2, -1, 1)
+    lax.fori_loop(0, blk_dev // 4, near_block, 0)
+    forward(3, 1, 1)
+    forward(3, -1, 1)
+    lax.fori_loop(blk_dev // 4, blk_dev // 2, near_block, 0)
+    forward(2, 1, 2)
+    forward(2, -1, 2)
+    lax.fori_loop(blk_dev // 2, blk_dev * 3 // 4, near_block, 0)
+    forward(3, 1, 2)
+    forward(3, -1, 2)
+    lax.fori_loop(blk_dev * 3 // 4, blk_dev, near_block, 0)
+    forward(2, 1, 3)
+    forward(2, -1, 3)
+    lax.fori_loop(0, count // 2, far2, 0, unroll=2)
+    forward(3, 1, 3)
+    forward(3, -1, 3)
+    lax.fori_loop(count // 2, count, far2, 0, unroll=2)
+    crossed(1, 1, 0)
+    for d, k in ways:
+        crossed(1, d, k)
+    lax.fori_loop(0, count, far1, 0, unroll=2)
+    for i in (2, 3):
+        crossed(i, 1, 0)
+    for d, k in ways:
+        for i in (2, 3):
+            crossed(i, d, k)
+
+    for m, mate in enumerate(mates):
+        def far0(p, c, m=m, mate=mate):
+            at = s_peer(*mate) * pairs + p
+            red_out[m, p] = (facc[at] + far_pair(0, at)).astype(jnp.bfloat16)
             return c
 
-        lax.fori_loop(0, pairs, far0, 0)
-        r_copy(j).start()
+        lax.fori_loop(0, pairs, far0, 0, unroll=2)
+        r_copy(m).start()
 
     def far_own(p, c):
         at = src * pairs + p
         facc[at] = facc[at] + far_pair(0, at)
         return c
 
-    lax.fori_loop(0, pairs, far_own, 0)
-    for j in range(1, n_src):
-        r_copy(j).wait_recv()
+    lax.fori_loop(0, pairs, far_own, 0, unroll=2)
+    for m in range(len(mates)):
+        r_copy(m).wait_recv()
 
     def last(p, c):
         total = facc[src * pairs + p]
-        for j in range(1, n_src):
-            total = total + red_in[j, p].astype(jnp.float32)
+        for m in range(len(mates)):
+            total = total + red_in[m, p].astype(jnp.float32)
         for h in range(2):
             rows = pl.ds(pl.multiple_of((2 * p + h) * BLK, BLK), BLK)
             out[rows, :] = out[rows, :] + total[:, h * WCOL : (h + 1) * WCOL]
@@ -260,15 +343,28 @@
 
     lax.fori_loop(0, pairs, last, 0)
 
-    for l in (2, 1, 0):
-        for k in range(1, Z):
-            z_copy(l, k).wait_send()
-        for k in range(Z):
-            for j in range(1, X):
-                x_copy(l, k, j).wait_send()
-    for k in range(1, n_src):
+    for i in range(4):
+        for j in range(1, X):
+            x_copy(i, 1, 0, j).wait_send()
+        for d, k in [(1, 0), (-1, 0)] + ways:
+            if k < Z - 1:
+                @pl.when(has(d, k) & more(d))
+                def _(i=i, d=d, k=k):
+                    z_copy(i, d, k, x, 0).wait_send()
+                    if i == 0:
+                        for j in range(1, X):
+                            z_copy(0, d, k, x_from(j), j).wait_send()
+            if k > 0 and i > 0:
+                @pl.when(has(d, k))
+                def _(i=i, d=d, k=k):
+                    for j in range(1, X):
+                        x_copy(i, d, k, j).wait_send()
+    for k in range(1, Y):
         g_copy(k).wait_send()
-        r_copy(k).wait_send()
+    for k in range(Y):
+        c_copy(k).wait_send()
+    for m in range(len(mates)):
+        r_copy(m).wait_send()
 
 
 def shards(n_tgt, n_src, points, weights, near_list, far_list, skel_index, equiv_weights):
@@ -294,8 +390,8 @@
             pltpu.VMEM((n_src, blk_dev // 2, BLK, 2 * WCOL), bf16),
             pltpu.VMEM((n_src, blk_dev // 2, BLK, 2 * WCOL), bf16),
             dma((n_src,)), dma((n_src,)),
-            dma((LEVELS * Z,)), dma((LEVELS * Z,)),
-            dma((LEVELS * Z * X,)), dma((LEVELS * Z * X,)),
+            dma((8 * Z * X,)), dma((8 * Z * X,)),
+            dma((8 * Z * X,)), dma((8 * Z * X,)),
             dma((n_src,)), dma((n_src,)),
         ],
         compiler_params=pltpu.CompilerParams(

time: 191 us -> 154 us (0.81)
  the two profiles are of different devices: /device:TPU:9 before, /device:TPU:1 now
where the time goes in v2:
time: 154 us; the launch traced here: 153 us
  Pallas kernels  145 us (94%)
  local copies, waits for them, and re-layouts  8.08 us (5%)
    pallas_call x1, Pallas kernels, shards(): pl.pallas_call(functools.partial(kernel, n_tgt, n_src, blk_dev, level_nod...  145 us
    unnamed x6, local copies, waits for them, and re-layouts  5.75 us

profile of v2, /device:TPU:1, one launch (start us, length us, event | category | flops | bytes accessed | tf_op | source)
XLA Modules:
  0.0 153.3 jit_solution(11035753947187818962)
XLA Ops:
  0.0 1.3 copy.13
  1.3 1.5 copy.7
  2.8 0.0 copy-start
  2.8 2.0 %copy.9.ew = bf16[7,256,64]{2,1,0:T(8,128)(2,1)} copy(bf16[7,256,64]{1,2,0:T(8,128)(2,1)} %param.11) | data formatting | bytes 458752 | tf_op args[5]
  4.7 0.0 copy-done
  4.7 1.0 copy.8.wts
  5.7 145.2 %shard_map.64 = f32[2048,64]{1,0:T(8,128)} custom-call(bf16[2048,256]{1,0:T(8,128)(2,1)} %pts.1, bf16[2048,64]{1,0:T(8,128)(2,1)} %copy.8.wts, s32[256,7]{1,0:T(8,128)} %bitcast.6, bf16[7,256,64]{2,1,0:T(8,128)(2,1)} %copy.9.ew, s32[16,16]{1,0:T(8,128)} %near.1, s32[3,64]{1,0:T(4,128)} %bitcast.7), custom_call_target="tpu_custom_call" | custom-call | tf_op jit(solution)/shard_map/pallas_call | solution.py:379
  150.9 2.3 %copy.10 = f32[2048,64]{0,1:T(8,128)} copy(f32[2048,64]{1,0:T(8,128)} %shard_map.64) | data formatting | bytes 1048576 | tf_op jit(solution)/shard_map/pallas_call | solution.py:379
Async XLA Ops:
  2.8 2.0 %copy-start = (bf16[2048,64]{0,1:T(8,128)(2,1)S(1)}, bf16[2048,64]{0,1:T(8,128)(2,1)}, u32[]{:S(2)}) copy-start(bf16[2048,64]{0,1:T(8,128)(2,1)} %param.7) | copy-start | bytes 786436

commit v3 on v2

--- a/solution.py
+++ b/solution.py
@@ -64,8 +64,8 @@
     y, core = src // 2, src % 2
     levels, norms = (l0, l1, l2), (n0, n1, n2)
     pairs = blk_dev // 2
-    half0 = level_nodes[0] // 2
-    items = ((2, 0, level_nodes[2]), (1, 0, level_nodes[1]), (0, 0, half0), (0, half0, half0))
+    part0 = level_nodes[0] // 4
+    items = ((2, 0, level_nodes[2]), (1, 0, level_nodes[1]), *((0, q * part0, part0) for q in range(4)))
     mates = [(dy, dc) for dy in range(1, Y) for dc in range(2)] + [(0, 1)]
 
     def x_peer(j):
@@ -208,7 +208,8 @@
             def _(d=d, j=j):
                 z_copy(0, d, 0, x_from(j), j).start()
     gather_level(0)
-    send_own(2)
+    for i in range(2, len(items)):
+        send_own(i)
 
     def pack_block(b, c):
         at = src * blk_dev + b
@@ -220,7 +221,7 @@
     for k in range(1, Y):
         g_copy(k).start()
     c_copy(0).start()
-    for i in range(4):
+    for i in range(len(items)):
         item_norms(i, tgt)
     for j in range(1, X):
         item_norms(0, z * X + x_from(j))
@@ -233,7 +234,6 @@
         for d in (1, -1):
             forward_other(d, k)
         if k == 1:
-            send_own(3)
             for j in range(1, Y):
                 g_copy(j).wait_recv()
                 c_copy(j).start()
@@ -286,32 +286,38 @@
         return c
 
     count = n_src * pairs
-    forward(2, 1, 1)
-    forward(2, -1, 1)
+    for i in (2, 3):
+        forward(i, 1, 1)
+        forward(i, -1, 1)
     lax.fori_loop(0, blk_dev // 4, near_block, 0)
-    forward(3, 1, 1)
-    forward(3, -1, 1)
+    for i in (4, 5):
+        forward(i, 1, 1)
+        forward(i, -1, 1)
     lax.fori_loop(blk_dev // 4, blk_dev // 2, near_block, 0)
-    forward(2, 1, 2)
-    forward(2, -1, 2)
+    for i in (2, 3):
+        forward(i, 1, 2)
+        forward(i, -1, 2)
     lax.fori_loop(blk_dev // 2, blk_dev * 3 // 4, near_block, 0)
-    forward(3, 1, 2)
-    forward(3, -1, 2)
+    for i in (4, 5):
+        forward(i, 1, 2)
+        forward(i, -1, 2)
     lax.fori_loop(blk_dev * 3 // 4, blk_dev, near_block, 0)
-    forward(2, 1, 3)
-    forward(2, -1, 3)
+    for i in (2, 3):
+        forward(i, 1, 3)
+        forward(i, -1, 3)
     lax.fori_loop(0, count // 2, far2, 0, unroll=2)
-    forward(3, 1, 3)
-    forward(3, -1, 3)
+    for i in (4, 5):
+        forward(i, 1, 3)
+        forward(i, -1, 3)
     lax.fori_loop(count // 2, count, far2, 0, unroll=2)
     crossed(1, 1, 0)
     for d, k in ways:
         crossed(1, d, k)
     lax.fori_loop(0, count, far1, 0, unroll=2)
-    for i in (2, 3):
+    for i in range(2, 6):
         crossed(i, 1, 0)
     for d, k in ways:
-        for i in (2, 3):
+        for i in range(2, 6):
             crossed(i, d, k)
 
     for m, mate in enumerate(mates):
@@ -320,7 +326,7 @@
             red_out[m, p] = (facc[at] + far_pair(0, at)).astype(jnp.bfloat16)
             return c
 
-        lax.fori_loop(0, pairs, far0, 0, unroll=2)
+        lax.fori_loop(0, pairs, far0, 0, unroll=4)
         r_copy(m).start()
 
     def far_own(p, c):
@@ -328,7 +334,7 @@
         facc[at] = facc[at] + far_pair(0, at)
         return c
 
-    lax.fori_loop(0, pairs, far_own, 0, unroll=2)
+    lax.fori_loop(0, pairs, far_own, 0, unroll=4)
     for m in range(len(mates)):
         r_copy(m).wait_recv()
 
@@ -343,7 +349,7 @@
 
     lax.fori_loop(0, pairs, last, 0)
 
-    for i in range(4):
+    for i in range(len(items)):
         for j in range(1, X):
             x_copy(i, 1, 0, j).wait_send()
         for d, k in [(1, 0), (-1, 0)] + ways:
@@ -390,8 +396,8 @@
             pltpu.VMEM((n_src, blk_dev // 2, BLK, 2 * WCOL), bf16),
             pltpu.VMEM((n_src, blk_dev // 2, BLK, 2 * WCOL), bf16),
             dma((n_src,)), dma((n_src,)),
-            dma((8 * Z * X,)), dma((8 * Z * X,)),
-            dma((8 * Z * X,)), dma((8 * Z * X,)),
+            dma((12 * Z * X,)), dma((12 * Z * X,)),
+            dma((12 * Z * X,)), dma((12 * Z * X,)),
             dma((n_src,)), dma((n_src,)),
         ],
         compiler_params=pltpu.CompilerParams(

time: 154 us -> 157 us (1.019)
  Pallas kernels: 145 us -> 149 us
    pallas_call x1, Pallas kernels: 145 us -> 149 us  [shards(): pl.pallas_call(functools.partial(kernel, n_tgt, n_src, blk_dev, level_nod...]
where the time goes in v3:
time: 157 us
  Pallas kernels  149 us (95%)
  local copies, waits for them, and re-layouts  8.08 us (5%)
    pallas_call x1, Pallas kernels, shards(): pl.pallas_call(functools.partial(kernel, n_tgt, n_src, blk_dev, level_nod...  149 us
    unnamed x6, local copies, waits for them, and re-layouts  5.75 us

profile of v3, /device:TPU:1, one launch (start us, length us, event | category | flops | bytes accessed | tf_op | source)
XLA Modules:
  0.0 156.9 jit_solution(5050709921943590139)
XLA Ops:
  0.0 1.3 copy.13
  1.3 1.5 copy.7
  2.8 0.0 copy-start
  2.8 2.0 %copy.9.ew = bf16[7,256,64]{2,1,0:T(8,128)(2,1)} copy(bf16[7,256,64]{1,2,0:T(8,128)(2,1)} %param.11) | data formatting | bytes 458752 | tf_op args[5]
  4.7 0.0 copy-done
  4.7 1.0 copy.8.wts
  5.7 148.8 %shard_map.64 = f32[2048,64]{1,0:T(8,128)} custom-call(bf16[2048,256]{1,0:T(8,128)(2,1)} %pts.1, bf16[2048,64]{1,0:T(8,128)(2,1)} %copy.8.wts, s32[256,7]{1,0:T(8,128)} %bitcast.6, bf16[7,256,64]{2,1,0:T(8,128)(2,1)} %copy.9.ew, s32[16,16]{1,0:T(8,128)} %near.1, s32[3,64]{1,0:T(4,128)} %bitcast.7), custom_call_target="tpu_custom_call" | custom-call | tf_op jit(solution)/shard_map/pallas_call | solution.py:385
  154.5 2.3 %copy.10 = f32[2048,64]{0,1:T(8,128)} copy(f32[2048,64]{1,0:T(8,128)} %shard_map.64) | data formatting | bytes 1048576 | tf_op jit(solution)/shard_map/pallas_call | solution.py:385
Async XLA Ops:
  2.8 2.0 %copy-start = (bf16[2048,64]{0,1:T(8,128)(2,1)S(1)}, bf16[2048,64]{0,1:T(8,128)(2,1)}, u32[]{:S(2)}) copy-start(bf16[2048,64]{0,1:T(8,128)(2,1)} %param.7) | copy-start | bytes 786436
